TPU v7x, 32 devices: a whole 2x2x4 slice. The times are simulated.
32 devices in a mesh: groups: 2 (over y), gx: 16 (over z, x, core).
Axes of the slice: x: 2, y: 2, z: 4, core: 2. Of those that a mesh axis runs over, the one named last changes fastest.
Arguments:
- states: float32 [2, 4, 128, 512], P(None, 'groups', 'gx'), parts along dimension 1, may hold values from -5 to 5
- pre_acts: bfloat16 [2, 3, 256, 48, 512], P(None, None, ('groups', 'gx')), parts along dimension 2, may hold values from -6 to 6
- cotangent: float32 [4, 128, 512], P('groups', 'gx'), parts along dimension 0, may hold values from -12 to 12
- weight_in: bfloat16 [9, 48, 2], replicated, may hold values from -1.5 to 1.5
- weight_second: bfloat16 [9, 48, 48], replicated, may hold values from -0.3125 to 0.3125
- weight_third: bfloat16 [9, 48, 48], replicated, may hold values from -0.3125 to 0.3125
- weight_out: bfloat16 [9, 2, 48], replicated, may hold values from -0.3125 to 0.3125
Outputs:
- state_adjoint: float32 [4, 128, 512], P('groups', 'gx'), parts along dimension 0
- grad_in: float32 [18, 48, 2], P('groups'), parts along dimension 0
- grad_second: float32 [18, 48, 48], P('groups'), parts along dimension 0
- grad_third: float32 [18, 48, 48], P('groups'), parts along dimension 0
- grad_out: float32 [18, 2, 48], P('groups'), parts along dimension 0
There are 2 independent parts, one for each index of `groups`. A program takes and returns all parts, laid end to end along the dimension named above; an argument that names none is the same for every part. Nothing has to cross between parts.
All inputs are finite; a program needn't handle non-finite values.
Results may differ from a plain program's by a relative error of at most 0.0065.
Values may be sent and summed in bfloat16 or wider, within the bound.
A program may use at most 64 MiB of HBM per device.

v0:
```python
import math

import jax
import jax.numpy as jnp
from jax import lax
from jax.sharding import PartitionSpec as P

step_factor = 0.25
viscosity = 0.4


def extended(cells, sides, width):
    for axis, dim in sides:
        count = lax.axis_size(axis)
        head = lax.slice_in_dim(cells, 0, width, axis=dim)
        tail = lax.slice_in_dim(cells, cells.shape[dim] - width, cells.shape[dim], axis=dim)
        cells = jnp.concatenate(
            [
                lax.ppermute(tail, axis, [(i, (i + 1) % count) for i in range(count)]),
                cells,
                lax.ppermute(head, axis, [((i + 1) % count, i) for i in range(count)]),
            ],
            axis=dim,
        )
    return cells


def trim_rows(values, rim_width):
    return values[:, rim_width : values.shape[1] - rim_width]


def trim_lead(values, rim_width):
    return values[rim_width : values.shape[0] - rim_width]


def half_valid(state_ext):
    row_count = state_ext.shape[1] - 2
    row_speed = state_ext[0]
    col_speed = state_ext[1][1 : row_count + 1]
    face_speed = 0.25 * (row_speed[:-1] + row_speed[1:])
    side_speed = 0.25 * (col_speed + jnp.roll(col_speed, -1, axis=-1))
    outputs = []
    for component in range(2):
        values = state_ext[component]
        middle = values[1 : row_count + 1]
        row_flux = face_speed * (values[:-1] + values[1:])
        col_flux = side_speed * (middle + jnp.roll(middle, -1, axis=-1))
        divergence = row_flux[1:] - row_flux[:-1] + (col_flux - jnp.roll(col_flux, 1, axis=-1))
        laplacian = (
            values[2:]
            + values[:-2]
            + jnp.roll(middle, -1, axis=-1)
            + jnp.roll(middle, 1, axis=-1)
            - 4.0 * middle
        )
        outputs.append(middle + step_factor * (viscosity * laplacian - divergence))
    return jnp.stack(outputs)


def relu_value(preact):
    return jnp.maximum(preact.astype(jnp.float32), jnp.float32(0.0))


def relu_slope(preact):
    return jnp.where(preact > 0, jnp.float32(1.0), jnp.float32(0.0))


def col_shifts(values):
    return [jnp.roll(values, 1, axis=-1), values, jnp.roll(values, -1, axis=-1)]


def weight_terms(gradient, source_ext):
    row_count = gradient.shape[0]
    shifted = col_shifts(source_ext)
    products = []
    for row_tap in range(3):
        for col_tap in range(3):
            section = shifted[col_tap][row_tap : row_tap + row_count]
            products.append(
                jnp.einsum("roy,rky->ok", gradient, section, preferred_element_type=jnp.float32)
            )
    return jnp.stack(products)


def back_conv(grad_ext, kernel):
    row_count = grad_ext.shape[0] - 2
    shifted = col_shifts(grad_ext)
    summed = None
    for row_tap in range(3):
        for col_tap in range(3):
            section = shifted[2 - col_tap][2 - row_tap : 2 - row_tap + row_count]
            product = jnp.einsum(
                "ok,roy->rky",
                kernel[3 * row_tap + col_tap],
                section,
                preferred_element_type=jnp.float32,
            )
            summed = product if summed is None else summed + product
    return summed


def gradient_rim(gradient):
    return extended(gradient, (("gx", 0),), 1)


def layer_step(state, preacts, adjoint, kernels, grad_totals):
    channels = preacts.shape[2]
    state_ext = extended(state, (("gx", 1),), 2)
    half_ext, pullback = jax.vjp(half_valid, state_ext)
    source_first = jnp.swapaxes(half_ext, 0, 1).astype(jnp.bfloat16)
    gradient = jnp.swapaxes(adjoint, 0, 1).astype(jnp.bfloat16)
    backward = None
    for layer_index in (3, 2, 1, 0):
        if layer_index > 0:
            joined = extended(
                jnp.concatenate([preacts[layer_index - 1], gradient], axis=1), (("gx", 0),), 1
            )
            preact_ext = joined[:, :channels]
            grad_ext = joined[:, channels:]
            source = relu_value(preact_ext).astype(jnp.bfloat16)
        else:
            grad_ext = gradient_rim(gradient)
            source = source_first
        grad_totals[layer_index] = grad_totals[layer_index] + weight_terms(gradient, source)
        backward = back_conv(grad_ext, kernels[layer_index])
        if layer_index > 0:
            gradient = (backward * relu_slope(trim_lead(preact_ext, 1))).astype(jnp.bfloat16)
    combined = adjoint + jnp.swapaxes(backward, 0, 1)
    combined_ext = extended(combined, (("gx", 1),), 1)
    return (trim_rows(pullback(combined_ext)[0], 2), grad_totals)


def on_device(states, pre_acts, cotangent, weight_in, weight_second, weight_third, weight_out):
    kernels = (weight_in, weight_second, weight_third, weight_out)
    grad_totals = [jnp.zeros(kernel.shape, jnp.float32) for kernel in kernels]
    adjoint = cotangent
    for step_index in (1, 0):
        adjoint, grad_totals = layer_step(
            states[step_index], pre_acts[step_index], adjoint, kernels, grad_totals
        )
    summed = lax.psum((grad_totals[0], grad_totals[1], grad_totals[2], grad_totals[3]), "gx")
    factor = 1.0 / math.sqrt(cotangent.shape[1] * lax.axis_size("gx") * cotangent.shape[2])
    return (adjoint, summed[0] * factor, summed[1] * factor, summed[2] * factor, summed[3] * factor)


def solution(mesh):
    return jax.shard_map(
        on_device,
        mesh=mesh,
        in_specs=(
            P(None, "groups", "gx", None),
            P(None, None, ("groups", "gx"), None, None),
            P("groups", "gx", None),
            P(),
            P(),
            P(),
            P(),
        ),
        out_specs=(
            P("groups", "gx", None),
            P("groups", None, None),
            P("groups", None, None),
            P("groups", None, None),
            P("groups", None, None),
        ),
        check_vma=False,
    )
```

profile of v0, /device:TPU:1, one launch (start us, length us, event | category | flops | bytes accessed | tf_op | source)
XLA Modules:
  0.0 229.7 jit_solution(16800260987941374135)
XLA Ops:
  7.2 0.8 convert_element_type.98
  8.0 1.9 slice_bitcast_fusion.2
  9.9 2.7 %collective-permute-start = (bf16[1,50,512]{2,1,0:T(8,128)(2,1)S(1)}, bf16[1,50,512]{2,1,0:T(8,128)(2,1)S(1)}, u32[]{:S(2)}, u32[]{:S(2)}) collective-permute-start(bf16[1,50,512]{2,1,0:T(8,128)(2,1)S(1)} %get-tuple-element.85), channel_id=1, source_target_pairs={{0,1},{1,2},{2,3},{3,4},{4,5},{5,6},{6,7},{7,8},{8,9},{9,10},{10,1... | collective-permute-start | bytes 153608 | tf_op jit(solution)/shard_map/ppermute | solution.py:19
  12.6 1.8 collective-permute-start.10
  14.4 1.3 collective-permute-start.11
  15.7 0.5 collective-permute-start.22
  16.5 4.9 %collective-permute-start.23 = (f32[2,2,512]{2,1,0:T(2,128)S(1)}, f32[2,2,512]{2,1,0:T(2,128)S(1)}, u32[]{:S(2)}, u32[]{:S(2)}) collective-permute-start(f32[2,2,512]{2,1,0:T(2,128)S(1)} %get-tuple-element.189), channel_id=1, source_target_pairs={{1,0},{2,1},{3,2},{4,3},{5,4},{6,5},{7,6},{8,7},{9,8},{10,9},{11,1... | collective-permute-start | bytes 24584 | tf_op jit(solution)/shard_map/ppermute | solution.py:21
  21.7 0.5 collective-permute-done.23
  25.3 0.5 fusion.15
  26.1 1.6 fusion.28
  27.8 4.1 %collective-permute-start.3 = (bf16[1,96,512]{2,1,0:T(8,128)(2,1)S(1)}, bf16[1,96,512]{2,1,0:T(8,128)(2,1)S(1)}, u32[]{:S(2)}, u32[]{:S(2)}) collective-permute-start(bf16[1,96,512]{2,1,0:T(8,128)(2,1)S(1)} %get-tuple-element.46), channel_id=1, source_target_pairs={{1,0},{2,1},{3,2},{4,3},{5,4},{6,5},{7,6},{8,7},{9,8},{10,9},{11,1... | collective-permute-start | bytes 294920 | tf_op jit(solution)/shard_map/ppermute | solution.py:21
  34.3 2.8 %collective-permute-done.2 = bf16[1,96,512]{2,1,0:T(8,128)(2,1)S(1)} collective-permute-done((bf16[1,96,512]{2,1,0:T(8,128)(2,1)S(1)}, bf16[1,96,512]{2,1,0:T(8,128)(2,1)S(1)}, u32[]{:S(2)}, u32[]{:S(2)}) %collective-permute-start.2) | collective-permute-done | bytes 98336 | tf_op jit(solution)/shard_map/ppermute | solution.py:19
  37.8 0.4 fusion.117
  38.2 0.4 copy-done
  41.3 6.1 %collective-permute-start.5 = (bf16[1,96,512]{2,1,0:T(8,128)(2,1)S(1)}, bf16[1,96,512]{2,1,0:T(8,128)(2,1)S(1)}, u32[]{:S(2)}, u32[]{:S(2)}) collective-permute-start(bf16[1,96,512]{2,1,0:T(8,128)(2,1)S(1)} %get-tuple-element.44), channel_id=1, source_target_pairs={{1,0},{2,1},{3,2},{4,3},{5,4},{6,5},{7,6},{8,7},{9,8},{10,9},{11,1... | collective-permute-start | bytes 294920 | tf_op jit(solution)/shard_map/ppermute | solution.py:21
  47.4 0.3 fusion.55
  47.9 0.3 fusion.53
  48.3 0.3 fusion.52
  48.8 0.3 fusion.50
  49.2 0.3 fusion.49
  49.7 0.3 fusion.47
  50.9 0.4 fusion.115
  51.2 0.4 copy-done.1
  54.3 1.4 collective-permute-start.6
  55.7 3.0 %collective-permute-start.7 = (bf16[1,48,512]{2,1,0:T(8,128)(2,1)S(1)}, bf16[1,48,512]{2,1,0:T(8,128)(2,1)S(1)}, u32[]{:S(2)}, u32[]{:S(2)}) collective-permute-start(bf16[1,48,512]{2,1,0:T(8,128)(2,1)S(1)} %get-tuple-element.90), channel_id=1, source_target_pairs={{1,0},{2,1},{3,2},{4,3},{5,4},{6,5},{7,6},{8,7},{9,8},{10,9},{11,1... | collective-permute-start | bytes 147464 | tf_op jit(solution)/shard_map/ppermute | solution.py:21
  58.7 0.3 fusion.73
  59.3 0.3 fusion.71
  59.6 0.3 fusion.70
  60.3 0.3 fusion.68
  60.6 0.3 fusion.67
  63.9 4.4 %collective-permute-start.9 = (f32[2,1,512]{2,1,0:T(1,128)S(1)}, f32[2,1,512]{2,1,0:T(1,128)S(1)}, u32[]{:S(2)}, u32[]{:S(2)}) collective-permute-start(f32[2,1,512]{2,1,0:T(1,128)S(1)} %get-tuple-element.185), channel_id=1, source_target_pairs={{1,0},{2,1},{3,2},{4,3},{5,4},{6,5},{7,6},{8,7},{9,8},{10,9},{11,1... | collective-permute-start | bytes 12296 | tf_op jit(solution)/shard_map/ppermute | solution.py:21
  71.0 4.9 %collective-permute-start.13 = (bf16[1,50,512]{2,1,0:T(8,128)(2,1)S(1)}, bf16[1,50,512]{2,1,0:T(8,128)(2,1)S(1)}, u32[]{:S(2)}, u32[]{:S(2)}) collective-permute-start(bf16[1,50,512]{2,1,0:T(8,128)(2,1)S(1)} %get-tuple-element.84), channel_id=1, source_target_pairs={{1,0},{2,1},{3,2},{4,3},{5,4},{6,5},{7,6},{8,7},{9,8},{10,9},{11,1... | collective-permute-start | bytes 153608 | tf_op jit(solution)/shard_map/ppermute | solution.py:21
  78.0 3.1 %collective-permute-done.12 = bf16[1,50,512]{2,1,0:T(8,128)(2,1)S(1)} collective-permute-done((bf16[1,50,512]{2,1,0:T(8,128)(2,1)S(1)}, bf16[1,50,512]{2,1,0:T(8,128)(2,1)S(1)}, u32[]{:S(2)}, u32[]{:S(2)}) %collective-permute-start.12) | collective-permute-done | bytes 51232 | tf_op jit(solution)/shard_map/ppermute | solution.py:19
  83.2 0.5 fusion.7
  84.0 1.6 fusion.29
  85.7 5.8 %collective-permute-start.15 = (bf16[1,96,512]{2,1,0:T(8,128)(2,1)S(1)}, bf16[1,96,512]{2,1,0:T(8,128)(2,1)S(1)}, u32[]{:S(2)}, u32[]{:S(2)}) collective-permute-start(bf16[1,96,512]{2,1,0:T(8,128)(2,1)S(1)} %get-tuple-element.42), channel_id=1, source_target_pairs={{1,0},{2,1},{3,2},{4,3},{5,4},{6,5},{7,6},{8,7},{9,8},{10,9},{11,1... | collective-permute-start | bytes 294920 | tf_op jit(solution)/shard_map/ppermute | solution.py:21
  94.8 0.3 fusion.46
  95.4 0.3 fusion.44
  95.7 0.3 fusion.43
  96.3 0.3 fusion.41
  96.7 0.3 fusion.40
  97.2 0.4 fusion.113
  99.9 0.3 fusion.32
  100.4 4.2 %collective-permute-start.17 = (bf16[1,96,512]{2,1,0:T(8,128)(2,1)S(1)}, bf16[1,96,512]{2,1,0:T(8,128)(2,1)S(1)}, u32[]{:S(2)}, u32[]{:S(2)}) collective-permute-start(bf16[1,96,512]{2,1,0:T(8,128)(2,1)S(1)} %get-tuple-element.40), channel_id=1, source_target_pairs={{1,0},{2,1},{3,2},{4,3},{5,4},{6,5},{7,6},{8,7},{9,8},{10,9},{11,1... | collective-permute-start | bytes 294920 | tf_op jit(solution)/shard_map/ppermute | solution.py:21
  104.9 0.7 add.662
  106.4 0.3 fusion.64
  107.0 0.3 fusion.62
  107.3 0.3 fusion.61
  107.9 0.3 fusion.59
  108.2 0.3 fusion.58
  108.8 0.4 fusion.111
  111.9 5.7 %collective-permute-start.19 = (bf16[1,48,512]{2,1,0:T(8,128)(2,1)S(1)}, bf16[1,48,512]{2,1,0:T(8,128)(2,1)S(1)}, u32[]{:S(2)}, u32[]{:S(2)}) collective-permute-start(bf16[1,48,512]{2,1,0:T(8,128)(2,1)S(1)} %get-tuple-element.88), channel_id=1, source_target_pairs={{1,0},{2,1},{3,2},{4,3},{5,4},{6,5},{7,6},{8,7},{9,8},{10,9},{11,1... | collective-permute-start | bytes 147464 | tf_op jit(solution)/shard_map/ppermute | solution.py:21
  117.8 0.5 collective-permute-done.18
  119.7 0.3 convolution_add_fusion.36
  120.2 0.3 convolution_add_fusion.34
  121.0 5.4 %collective-permute-start.21 = (f32[2,1,512]{2,0,1:T(2,128)S(1)}, f32[2,1,512]{2,0,1:T(2,128)S(1)}, u32[]{:S(2)}, u32[]{:S(2)}) collective-permute-start(f32[2,1,512]{2,0,1:T(2,128)S(1)} %get-tuple-element.175), channel_id=1, source_target_pairs={{1,0},{2,1},{3,2},{4,3},{5,4},{6,5},{7,6},{8,7},{9,8},{10,9},{11,1... | collective-permute-start | bytes 12296 | tf_op jit(solution)/shard_map/ppermute | solution.py:21
  126.7 0.7 add.661
  130.8 61.7 %all-reduce.78 = (f32[9,48,2]{1,2,0:T(2,128)S(1)}, f32[9,2,48]{2,1,0:T(2,128)S(1)}) all-reduce(f32[9,48,2]{1,2,0:T(2,128)S(1)} %add.660, f32[9,2,48]{2,1,0:T(2,128)S(1)} %add.663), channel_id=1, replica_groups=mesh['groups'=2,'gx'=16] {'gx'}, use_global_device_ids=true, to_apply=%region_0.1 | all-reduce | flops 1728 | bytes 13824 | tf_op jit(solution)/shard_map/psum | solution.py:141
  192.4 0.6 broadcast_multiply_fusion.2
  193.0 0.6 broadcast_multiply_fusion.3
  194.0 0.6 pad_add_fusion
  194.7 24.9 %all-reduce.82.cloned.1.call-done = (f32[9,48,48]{2,1,0:T(8,128)}, f32[9,48,48]{2,1,0:T(8,128)}) async-done(((f32[9,48,48]{2,1,0:T(8,128)}, f32[9,48,48]{2,1,0:T(8,128)}), (f32[9,48,48]{2,1,0:T(8,128)}, f32[9,48,48]{2,1,0:T(8,128)})) %all-reduce.82.cloned.1.call-update) | async-done | bytes 165904 | tf_op jit(solution)/shard_map/psum | solution.py:141
  219.5 1.6 broadcast_multiply_fusion
  221.2 1.6 broadcast_multiply_fusion.1
  (288 shorter events, 41.2 us)
Async XLA Ops:
  7.2 212.4 %all-reduce.82.cloned.1.call-start = ((), (), s32[]{:S(2)}) async-start(), calls=%async_computation | async-start | bytes 884736 | tf_op jit(solution)/shard_map/psum | solution.py:141
  8.0 4.6 %copy-start.3 = (f32[2,2,8,512]{3,2,1,0:T(8,128)S(1)}, f32[2,2,8,512]{3,2,1,0:T(8,128)}, u32[]{:S(2)}) copy-start(f32[2,2,8,512]{3,2,1,0:T(8,128)} %param.7) | copy-start | bytes 196612
  8.0 8.1 %copy-start.4 = (bf16[9,2,48]{2,1,0:T(2,128)(2,1)S(1)}, bf16[9,2,48]{2,1,0:T(2,128)(2,1)}, u32[]{:S(2)}) copy-start(bf16[9,2,48]{2,1,0:T(2,128)(2,1)} %param.13) | copy-start | bytes 5188
  9.9 13.2 %collective-permute-start = (bf16[1,50,512]{2,1,0:T(8,128)(2,1)S(1)}, bf16[1,50,512]{2,1,0:T(8,128)(2,1)S(1)}, u32[]{:S(2)}, u32[]{:S(2)}) collective-permute-start(bf16[1,50,512]{2,1,0:T(8,128)(2,1)S(1)} %get-tuple-element.85), channel_id=1, source_target_pairs={{0,1},{1,2},{2,3},{3,4},{4,5},{5,6},{6,7},{7,8},{8,9},{9,10},{10,1... | collective-permute-start | bytes 153608 | tf_op jit(solution)/shard_map/ppermute | solution.py:19
  12.6 10.6 %collective-permute-start.1 = (bf16[1,50,512]{2,1,0:T(8,128)(2,1)S(1)}, bf16[1,50,512]{2,1,0:T(8,128)(2,1)S(1)}, u32[]{:S(2)}, u32[]{:S(2)}) collective-permute-start(bf16[1,50,512]{2,1,0:T(8,128)(2,1)S(1)} %get-tuple-element.86), channel_id=1, source_target_pairs={{1,0},{2,1},{3,2},{4,3},{5,4},{6,5},{7,6},{8,7},{9,8},{10,9},{11,1... | collective-permute-start | bytes 153608 | tf_op jit(solution)/shard_map/ppermute | solution.py:21
  12.6 3.9 %collective-permute-start.10 = (f32[2,2,512]{2,1,0:T(2,128)S(1)}, f32[2,2,512]{2,1,0:T(2,128)S(1)}, u32[]{:S(2)}, u32[]{:S(2)}) collective-permute-start(f32[2,2,512]{2,1,0:T(2,128)S(1)} %get-tuple-element.186), channel_id=1, source_target_pairs={{0,1},{1,2},{2,3},{3,4},{4,5},{5,6},{6,7},{7,8},{8,9},{9,10},{10,1... | collective-permute-start | bytes 24584 | tf_op jit(solution)/shard_map/ppermute | solution.py:19
  14.4 7.0 %collective-permute-start.11 = (f32[2,2,512]{2,1,0:T(2,128)S(1)}, f32[2,2,512]{2,1,0:T(2,128)S(1)}, u32[]{:S(2)}, u32[]{:S(2)}) collective-permute-start(f32[2,2,512]{2,1,0:T(2,128)S(1)} %get-tuple-element.187), channel_id=1, source_target_pairs={{1,0},{2,1},{3,2},{4,3},{5,4},{6,5},{7,6},{8,7},{9,8},{10,9},{11,1... | collective-permute-start | bytes 24584 | tf_op jit(solution)/shard_map/ppermute | solution.py:21
  15.7 6.1 %collective-permute-start.22 = (f32[2,2,512]{2,1,0:T(2,128)S(1)}, f32[2,2,512]{2,1,0:T(2,128)S(1)}, u32[]{:S(2)}, u32[]{:S(2)}) collective-permute-start(f32[2,2,512]{2,1,0:T(2,128)S(1)} %get-tuple-element.188), channel_id=1, source_target_pairs={{0,1},{1,2},{2,3},{3,4},{4,5},{5,6},{6,7},{7,8},{8,9},{9,10},{10,1... | collective-permute-start | bytes 24584 | tf_op jit(solution)/shard_map/ppermute | solution.py:19
  16.5 5.7 %collective-permute-start.23 = (f32[2,2,512]{2,1,0:T(2,128)S(1)}, f32[2,2,512]{2,1,0:T(2,128)S(1)}, u32[]{:S(2)}, u32[]{:S(2)}) collective-permute-start(f32[2,2,512]{2,1,0:T(2,128)S(1)} %get-tuple-element.189), channel_id=1, source_target_pairs={{1,0},{2,1},{3,2},{4,3},{5,4},{6,5},{7,6},{8,7},{9,8},{10,9},{11,1... | collective-permute-start | bytes 24584 | tf_op jit(solution)/shard_map/ppermute | solution.py:21
  27.8 6.5 %collective-permute-start.3 = (bf16[1,96,512]{2,1,0:T(8,128)(2,1)S(1)}, bf16[1,96,512]{2,1,0:T(8,128)(2,1)S(1)}, u32[]{:S(2)}, u32[]{:S(2)}) collective-permute-start(bf16[1,96,512]{2,1,0:T(8,128)(2,1)S(1)} %get-tuple-element.46), channel_id=1, source_target_pairs={{1,0},{2,1},{3,2},{4,3},{5,4},{6,5},{7,6},{8,7},{9,8},{10,9},{11,1... | collective-permute-start | bytes 294920 | tf_op jit(solution)/shard_map/ppermute | solution.py:21
  31.8 5.2 %collective-permute-start.2 = (bf16[1,96,512]{2,1,0:T(8,128)(2,1)S(1)}, bf16[1,96,512]{2,1,0:T(8,128)(2,1)S(1)}, u32[]{:S(2)}, u32[]{:S(2)}) collective-permute-start(bf16[1,96,512]{2,1,0:T(8,128)(2,1)S(1)} %get-tuple-element.45), channel_id=1, source_target_pairs={{0,1},{1,2},{2,3},{3,4},{4,5},{5,6},{6,7},{7,8},{8,9},{9,10},{10,1... | collective-permute-start | bytes 294920 | tf_op jit(solution)/shard_map/ppermute | solution.py:19
  37.7 0.9 copy-start
  41.3 8.8 %collective-permute-start.5 = (bf16[1,96,512]{2,1,0:T(8,128)(2,1)S(1)}, bf16[1,96,512]{2,1,0:T(8,128)(2,1)S(1)}, u32[]{:S(2)}, u32[]{:S(2)}) collective-permute-start(bf16[1,96,512]{2,1,0:T(8,128)(2,1)S(1)} %get-tuple-element.44), channel_id=1, source_target_pairs={{1,0},{2,1},{3,2},{4,3},{5,4},{6,5},{7,6},{8,7},{9,8},{10,9},{11,1... | collective-permute-start | bytes 294920 | tf_op jit(solution)/shard_map/ppermute | solution.py:21
  47.4 2.7 %collective-permute-start.4 = (bf16[1,96,512]{2,1,0:T(8,128)(2,1)S(1)}, bf16[1,96,512]{2,1,0:T(8,128)(2,1)S(1)}, u32[]{:S(2)}, u32[]{:S(2)}) collective-permute-start(bf16[1,96,512]{2,1,0:T(8,128)(2,1)S(1)} %get-tuple-element.43), channel_id=1, source_target_pairs={{0,1},{1,2},{2,3},{3,4},{4,5},{5,6},{6,7},{7,8},{8,9},{9,10},{10,1... | collective-permute-start | bytes 294920 | tf_op jit(solution)/shard_map/ppermute | solution.py:19
  50.8 0.9 copy-start.1
  54.3 7.0 %collective-permute-start.6 = (bf16[1,48,512]{2,1,0:T(8,128)(2,1)S(1)}, bf16[1,48,512]{2,1,0:T(8,128)(2,1)S(1)}, u32[]{:S(2)}, u32[]{:S(2)}) collective-permute-start(bf16[1,48,512]{2,1,0:T(8,128)(2,1)S(1)} %get-tuple-element.89), channel_id=1, source_target_pairs={{0,1},{1,2},{2,3},{3,4},{4,5},{5,6},{6,7},{7,8},{8,9},{9,10},{10,1... | collective-permute-start | bytes 147464 | tf_op jit(solution)/shard_map/ppermute | solution.py:19
  55.7 5.6 %collective-permute-start.7 = (bf16[1,48,512]{2,1,0:T(8,128)(2,1)S(1)}, bf16[1,48,512]{2,1,0:T(8,128)(2,1)S(1)}, u32[]{:S(2)}, u32[]{:S(2)}) collective-permute-start(bf16[1,48,512]{2,1,0:T(8,128)(2,1)S(1)} %get-tuple-element.90), channel_id=1, source_target_pairs={{1,0},{2,1},{3,2},{4,3},{5,4},{6,5},{7,6},{8,7},{9,8},{10,9},{11,1... | collective-permute-start | bytes 147464 | tf_op jit(solution)/shard_map/ppermute | solution.py:21
  60.0 1.2 copy-start.5
  62.5 1.2 copy-start.2
  63.8 5.1 %collective-permute-start.8 = (f32[2,1,512]{2,1,0:T(1,128)S(1)}, f32[2,1,512]{2,1,0:T(1,128)S(1)}, u32[]{:S(2)}, u32[]{:S(2)}) collective-permute-start(f32[2,1,512]{2,1,0:T(1,128)S(1)} %get-tuple-element.184), channel_id=1, source_target_pairs={{0,1},{1,2},{2,3},{3,4},{4,5},{5,6},{6,7},{7,8},{8,9},{9,10},{10,1... | collective-permute-start | bytes 12296 | tf_op jit(solution)/shard_map/ppermute | solution.py:19
  63.9 5.2 %collective-permute-start.9 = (f32[2,1,512]{2,1,0:T(1,128)S(1)}, f32[2,1,512]{2,1,0:T(1,128)S(1)}, u32[]{:S(2)}, u32[]{:S(2)}) collective-permute-start(f32[2,1,512]{2,1,0:T(1,128)S(1)} %get-tuple-element.185), channel_id=1, source_target_pairs={{1,0},{2,1},{3,2},{4,3},{5,4},{6,5},{7,6},{8,7},{9,8},{10,9},{11,1... | collective-permute-start | bytes 12296 | tf_op jit(solution)/shard_map/ppermute | solution.py:21
  71.0 7.0 %collective-permute-start.13 = (bf16[1,50,512]{2,1,0:T(8,128)(2,1)S(1)}, bf16[1,50,512]{2,1,0:T(8,128)(2,1)S(1)}, u32[]{:S(2)}, u32[]{:S(2)}) collective-permute-start(bf16[1,50,512]{2,1,0:T(8,128)(2,1)S(1)} %get-tuple-element.84), channel_id=1, source_target_pairs={{1,0},{2,1},{3,2},{4,3},{5,4},{6,5},{7,6},{8,7},{9,8},{10,9},{11,1... | collective-permute-start | bytes 153608 | tf_op jit(solution)/shard_map/ppermute | solution.py:21
  75.9 5.1 %collective-permute-start.12 = (bf16[1,50,512]{2,1,0:T(8,128)(2,1)S(1)}, bf16[1,50,512]{2,1,0:T(8,128)(2,1)S(1)}, u32[]{:S(2)}, u32[]{:S(2)}) collective-permute-start(bf16[1,50,512]{2,1,0:T(8,128)(2,1)S(1)} %get-tuple-element.83), channel_id=1, source_target_pairs={{0,1},{1,2},{2,3},{3,4},{4,5},{5,6},{6,7},{7,8},{8,9},{9,10},{10,1... | collective-permute-start | bytes 153608 | tf_op jit(solution)/shard_map/ppermute | solution.py:19
  85.7 8.4 %collective-permute-start.14 = (bf16[1,96,512]{2,1,0:T(8,128)(2,1)S(1)}, bf16[1,96,512]{2,1,0:T(8,128)(2,1)S(1)}, u32[]{:S(2)}, u32[]{:S(2)}) collective-permute-start(bf16[1,96,512]{2,1,0:T(8,128)(2,1)S(1)} %get-tuple-element.41), channel_id=1, source_target_pairs={{0,1},{1,2},{2,3},{3,4},{4,5},{5,6},{6,7},{7,8},{8,9},{9,10},{10,1... | collective-permute-start | bytes 294920 | tf_op jit(solution)/shard_map/ppermute | solution.py:19
  85.7 8.3 %collective-permute-start.15 = (bf16[1,96,512]{2,1,0:T(8,128)(2,1)S(1)}, bf16[1,96,512]{2,1,0:T(8,128)(2,1)S(1)}, u32[]{:S(2)}, u32[]{:S(2)}) collective-permute-start(bf16[1,96,512]{2,1,0:T(8,128)(2,1)S(1)} %get-tuple-element.42), channel_id=1, source_target_pairs={{1,0},{2,1},{3,2},{4,3},{5,4},{6,5},{7,6},{8,7},{9,8},{10,9},{11,1... | collective-permute-start | bytes 294920 | tf_op jit(solution)/shard_map/ppermute | solution.py:21
  100.3 5.3 %collective-permute-start.16 = (bf16[1,96,512]{2,1,0:T(8,128)(2,1)S(1)}, bf16[1,96,512]{2,1,0:T(8,128)(2,1)S(1)}, u32[]{:S(2)}, u32[]{:S(2)}) collective-permute-start(bf16[1,96,512]{2,1,0:T(8,128)(2,1)S(1)} %get-tuple-element.39), channel_id=1, source_target_pairs={{0,1},{1,2},{2,3},{3,4},{4,5},{5,6},{6,7},{7,8},{8,9},{9,10},{10,1... | collective-permute-start | bytes 294920 | tf_op jit(solution)/shard_map/ppermute | solution.py:19
  100.4 5.2 %collective-permute-start.17 = (bf16[1,96,512]{2,1,0:T(8,128)(2,1)S(1)}, bf16[1,96,512]{2,1,0:T(8,128)(2,1)S(1)}, u32[]{:S(2)}, u32[]{:S(2)}) collective-permute-start(bf16[1,96,512]{2,1,0:T(8,128)(2,1)S(1)} %get-tuple-element.40), channel_id=1, source_target_pairs={{1,0},{2,1},{3,2},{4,3},{5,4},{6,5},{7,6},{8,7},{9,8},{10,9},{11,1... | collective-permute-start | bytes 294920 | tf_op jit(solution)/shard_map/ppermute | solution.py:21
  111.9 6.5 %collective-permute-start.18 = (bf16[1,48,512]{2,1,0:T(8,128)(2,1)S(1)}, bf16[1,48,512]{2,1,0:T(8,128)(2,1)S(1)}, u32[]{:S(2)}, u32[]{:S(2)}) collective-permute-start(bf16[1,48,512]{2,1,0:T(8,128)(2,1)S(1)} %get-tuple-element.87), channel_id=1, source_target_pairs={{0,1},{1,2},{2,3},{3,4},{4,5},{5,6},{6,7},{7,8},{8,9},{9,10},{10,1... | collective-permute-start | bytes 147464 | tf_op jit(solution)/shard_map/ppermute | solution.py:19
  111.9 6.6 %collective-permute-start.19 = (bf16[1,48,512]{2,1,0:T(8,128)(2,1)S(1)}, bf16[1,48,512]{2,1,0:T(8,128)(2,1)S(1)}, u32[]{:S(2)}, u32[]{:S(2)}) collective-permute-start(bf16[1,48,512]{2,1,0:T(8,128)(2,1)S(1)} %get-tuple-element.88), channel_id=1, source_target_pairs={{1,0},{2,1},{3,2},{4,3},{5,4},{6,5},{7,6},{8,7},{9,8},{10,9},{11,1... | collective-permute-start | bytes 147464 | tf_op jit(solution)/shard_map/ppermute | solution.py:21
  120.9 6.5 %collective-permute-start.20 = (f32[2,1,512]{2,0,1:T(2,128)S(1)}, f32[2,1,512]{2,0,1:T(2,128)S(1)}, u32[]{:S(2)}, u32[]{:S(2)}) collective-permute-start(f32[2,1,512]{2,0,1:T(2,128)S(1)} %get-tuple-element.174), channel_id=1, source_target_pairs={{0,1},{1,2},{2,3},{3,4},{4,5},{5,6},{6,7},{7,8},{8,9},{9,10},{10,1... | collective-permute-start | bytes 12296 | tf_op jit(solution)/shard_map/ppermute | solution.py:19
  121.0 6.4 %collective-permute-start.21 = (f32[2,1,512]{2,0,1:T(2,128)S(1)}, f32[2,1,512]{2,0,1:T(2,128)S(1)}, u32[]{:S(2)}, u32[]{:S(2)}) collective-permute-start(f32[2,1,512]{2,0,1:T(2,128)S(1)} %get-tuple-element.175), channel_id=1, source_target_pairs={{1,0},{2,1},{3,2},{4,3},{5,4},{6,5},{7,6},{8,7},{9,8},{10,9},{11,1... | collective-permute-start | bytes 12296 | tf_op jit(solution)/shard_map/ppermute | solution.py:21
Sparse Core Ops, SparseCore 0:
  127.5 91.9 all-reduce.81
where the time goes:
time: 230 us
  blocking collectives  61.7 us (27%)
  starting transfers between devices  56.4 us (25%)
  matrix products  42.6 us (19%)
  waiting for transfers between devices  32.5 us (14%)
  between operations  15.5 us (7%)
  other arithmetic  11.9 us (5%)
  local copies, waits for them, and re-layouts  9.14 us (4%)
    psum x1, blocking collectives, on_device(): lax.psum((grad_totals[0], grad_totals[1], grad_totals[2], grad_totals[3])...  61.7 us
    ppermute x12, starting transfers between devices, extended(): lax.ppermute(head, axis, [((i + 1) % count, i) for i in range(count)])  49.8 us
    psum x1, waiting for transfers between devices, on_device(): lax.psum((grad_totals[0], grad_totals[1], grad_totals[2], grad_totals[3])...  24.9 us
    dot_general x72, matrix products, back_conv(): jnp.einsum('ok,roy->rky', kernel[3 * row_tap + col_tap], section, preferr...  23.2 us
    dot_general x72, matrix products, weight_terms(): jnp.einsum('roy,rky->ok', gradient, section, preferred_element_type=jnp.f...  19.4 us
    ppermute x12, waiting for transfers between devices, extended(): lax.ppermute(tail, axis, [(i, (i + 1) % count) for i in range(count)])  6.63 us
    ppermute x12, starting transfers between devices, extended(): lax.ppermute(tail, axis, [(i, (i + 1) % count) for i in range(count)])  6.61 us
  transfers between devices with their start and end apart: 25, of which 8 were waited for; matrix products, arithmetic and copies ran while one was open for 9% of the time, Pallas kernels for 0%

commit v1 on v0

v1 whole, which is shorter than its diff:
```python
import functools
import math

import jax
import jax.numpy as jnp
from jax import lax
from jax.experimental import pallas as pl
from jax.experimental.pallas import tpu as pltpu
from jax.sharding import PartitionSpec as P

step_factor = 0.25
viscosity = 0.4
lane_pad = 8
MESH = pl.DeviceIdType.MESH
IN_KERNEL_SUM = True


def roll_cols(values, amount):
    return pltpu.roll(values, amount % values.shape[-1], values.ndim - 1)


def roll_rows(values, amount):
    return pltpu.roll(values, amount % values.shape[-2], values.ndim - 2)


def east(values):
    return roll_cols(values, -1)


def west(values):
    return roll_cols(values, 1)


def south(values):
    return roll_rows(values, -1)


def north(values):
    return roll_rows(values, 1)


def half_step(row_speed, col_speed):
    face = 0.25 * (row_speed + south(row_speed))
    side = 0.25 * (col_speed + east(col_speed))
    outputs = []
    for values in (row_speed, col_speed):
        below, right = south(values), east(values)
        row_flux = face * (values + below)
        col_flux = side * (values + right)
        divergence = row_flux - north(row_flux) + (col_flux - west(col_flux))
        laplacian = below + north(values) + right + west(values) - 4.0 * values
        outputs.append(values + step_factor * (viscosity * laplacian - divergence))
    return outputs


def half_step_adjoint(row_speed, col_speed, grads):
    face = 0.25 * (row_speed + south(row_speed))
    side = 0.25 * (col_speed + east(col_speed))
    outputs = []
    face_grad = None
    side_grad = None
    for values, grad in zip((row_speed, col_speed), grads):
        below, right = south(grad), east(grad)
        row_part = step_factor * (below - grad)
        col_part = step_factor * (right - grad)
        laplacian = below + north(grad) + right + west(grad) - 4.0 * grad
        row_back = row_part * face
        col_back = col_part * side
        outputs.append(
            grad
            + (step_factor * viscosity) * laplacian
            + (row_back + north(row_back))
            + (col_back + west(col_back))
        )
        face_term = row_part * (values + south(values))
        side_term = col_part * (values + east(values))
        face_grad = face_term if face_grad is None else face_grad + face_term
        side_grad = side_term if side_grad is None else side_grad + side_term
    return [
        outputs[0] + 0.25 * (face_grad + north(face_grad)),
        outputs[1] + 0.25 * (side_grad + west(side_grad)),
    ]


def matmul(left, right):
    return lax.dot_general(left, right, (((1,), (0,)), ((), ())), preferred_element_type=jnp.float32)


def matmul_nt(left, right):
    return lax.dot_general(left, right, (((1,), (1,)), ((), ())), preferred_element_type=jnp.float32)


def kernel(
    count,
    pieces,
    scale,
    states,
    acts,
    cot,
    w_in,
    w_second,
    w_third,
    w_out,
    adj_out,
    sum_out,
    hal_u,
    hal_g,
    hal_a,
    hal_d,
    snd_d,
    grid_g,
    stage,
    wide,
    source,
    ghs,
    part,
    gathered,
    w2t,
    w3t,
    sem_u,
    sem_g,
    sem_a,
    sem_d,
    sem_rs,
    sem_ag,
):
    rows, cols = cot.shape[1], cot.shape[2]
    ch = acts.shape[3]
    me = lax.axis_index("gx")
    prev = lax.rem(me + count - 1, count)
    nxt = lax.rem(me + 1, count)

    barrier = pltpu.get_barrier_semaphore()
    if IN_KERNEL_SUM:

        def greet(k, carry):
            peer = lax.rem(me + k, count)
            pl.semaphore_signal(barrier, inc=1, device_id={"gx": peer}, device_id_type=MESH)
            return carry

        lax.fori_loop(1, count, greet, 0)
        pl.semaphore_wait(barrier, count - 1)
    else:
        for peer in (prev, nxt):
            pl.semaphore_signal(barrier, inc=1, device_id={"gx": peer}, device_id_type=MESH)
        pl.semaphore_wait(barrier, 2)

    def exchange(up_src, down_src, dst, sems):
        copies = []
        for src, side, peer in ((up_src, 1, prev), (down_src, 0, nxt)):
            copy = pltpu.make_async_remote_copy(
                src_ref=src,
                dst_ref=dst.at[side],
                send_sem=sems.at[0, side],
                recv_sem=sems.at[1, side],
                device_id={"gx": peer},
                device_id_type=MESH,
            )
            copy.start()
            copies.append(copy)
        return copies

    def arrived(copies):
        for copy in copies:
            copy.wait_recv()

    started = []
    cot_moves = exchange(cot, cot, hal_g.at[0], sem_g.at[0])
    act_moves = [None, None]
    act_moves[1] = exchange(acts.at[1, 2, 0], acts.at[1, 2, rows - 1], hal_a.at[1], sem_a.at[1])
    state_moves = exchange(states, states, hal_u, sem_u)
    act_moves[0] = exchange(acts.at[0, 2, 0], acts.at[0, 2, rows - 1], hal_a.at[0], sem_a.at[0])
    started += cot_moves + act_moves[0] + act_moves[1] + state_moves

    stage[...] = jnp.zeros_like(stage)
    source[...] = jnp.zeros_like(source)
    w2t[...] = jnp.transpose(w_second[...].astype(jnp.float32)).astype(jnp.bfloat16)
    w3t[...] = jnp.transpose(w_third[...].astype(jnp.float32)).astype(jnp.bfloat16)

    row_block = 3 * ch

    def put_row(buffer, row, values):
        place = (rows - row) * row_block
        wide[buffer, place : place + ch, :] = roll_cols(values, -1).astype(jnp.bfloat16)
        wide[buffer, place + ch : place + 2 * ch, :] = values.astype(jnp.bfloat16)
        wide[buffer, place + 2 * ch : place + 3 * ch, :] = roll_cols(values, 1).astype(jnp.bfloat16)

    def neighbourhood(buffer, row):
        place = (rows - 1 - row) * row_block
        return wide[buffer, place : place + 3 * row_block, :]

    def relu(values):
        return jnp.maximum(values.astype(jnp.float32), 0.0).astype(jnp.bfloat16)

    def masked(values, preact):
        kept = jnp.where(preact.astype(jnp.float32) > 0.0, values, 0.0)
        return kept.astype(jnp.bfloat16).astype(jnp.float32)

    def total(place, value, first):
        if first:
            part[place] = value
        else:
            part[place] = part[place] + value

    exchange_no = 0
    for step in (1, 0):
        first = step == 1
        if first:
            arrived(cot_moves)
            for comp in range(2):
                grid_g[comp, 0:rows, :] = hal_g[0, 0, comp]
                grid_g[comp, rows : 2 * rows, :] = cot[comp]
                grid_g[comp, 2 * rows : 3 * rows, :] = hal_g[0, 1, comp]
        for comp in range(2):
            values = grid_g[comp]
            for shift in range(3):
                moved = roll_cols(values, shift - 1) if shift != 1 else values
                for row in range(-2, rows + 2):
                    place = (rows + 1 - row) * 24 + shift * 8 + comp
                    stage[place : place + 1, :] = moved[row + rows : row + rows + 1, :]

        def stage_rows(row):
            place = (rows - row) * 24
            return stage[place : place + 72, :].astype(jnp.bfloat16)

        arrived(act_moves[step])
        for row in range(-1, rows + 1):
            if row < 0:
                preact = hal_a[step, 0]
            elif row >= rows:
                preact = hal_a[step, 1]
            else:
                preact = acts[step, 2, row]
            put_row(0, row, masked(matmul(w_out[...], stage_rows(row)), preact))

        def out_terms():
            acc = None
            for row in range(rows):
                term = matmul_nt(relu(acts[step, 2, row]), stage_rows(row))
                acc = term if acc is None else acc + term
            half = ch // 2
            total((pl.ds(2 * ch + 8, half), pl.ds(0, 72)), acc[:half], first)
            total((pl.ds(2 * ch + 8, half), pl.ds(128, 72)), acc[half:], first)

        def hidden_terms(layer, buffer):
            acc = None
            for row in range(rows):
                term = matmul_nt(relu(acts[step, layer, row]), neighbourhood(buffer, row))
                acc = term if acc is None else acc + term
            total((pl.ds(layer * ch, ch), pl.ds(0, 3 * row_block)), acc, first)

        for layer, kernel_t, buffer in ((1, w3t, 0), (0, w2t, 1)):
            target = 1 - buffer
            for row in (0, rows - 1):
                values = masked(matmul(kernel_t[...], neighbourhood(buffer, row)), acts[step, layer, row])
                snd_d[exchange_no, 0 if row == 0 else 1] = values.astype(jnp.bfloat16)
                put_row(target, row, values)
            moves = exchange(
                snd_d.at[exchange_no, 0], snd_d.at[exchange_no, 1], hal_d.at[exchange_no], sem_d.at[exchange_no]
            )
            started += moves
            for row in range(1, rows - 1):
                values = masked(matmul(kernel_t[...], neighbourhood(buffer, row)), acts[step, layer, row])
                put_row(target, row, values)
            if layer == 1:
                out_terms()
            hidden_terms(layer, buffer)
            if layer == 0:
                if first:
                    arrived(state_moves)
                speeds = [
                    jnp.concatenate(
                        [hal_u[0, step, comp], states[step, comp], hal_u[1, step, comp]], axis=0
                    )
                    for comp in range(2)
                ]
                halves = half_step(*speeds)
                for comp in range(2):
                    for row in range(rows):
                        place = row * 16 + comp
                        source[place : place + 1, :] = halves[comp][row + rows : row + rows + 1, :]
            arrived(moves)
            put_row(target, -1, hal_d[exchange_no, 0].astype(jnp.float32))
            put_row(target, rows, hal_d[exchange_no, 1].astype(jnp.float32))
            exchange_no += 1

        for row in range(rows):
            back = matmul(w_in[...], neighbourhood(0, row))
            for comp in range(2):
                ghs[1 - step, comp, row : row + 1, :] = (
                    back[comp : comp + 1] + grid_g[comp, rows + row : rows + row + 1, :]
                )
        slot = 1 + (1 - step)
        moves = exchange(ghs.at[1 - step], ghs.at[1 - step], hal_g.at[slot], sem_g.at[slot])
        started += moves
        acc = None
        for row in range(rows):
            term = matmul_nt(
                source[row * 16 : row * 16 + 16, :].astype(jnp.bfloat16), neighbourhood(0, row)
            )
            acc = term if acc is None else acc + term
        total((pl.ds(2 * ch, 8), pl.ds(0, 3 * row_block)), acc[:8], first)

        if step == 0 and IN_KERNEL_SUM:
            reducing = functools.partial(scatter_sum, count, pieces, me, part, gathered, sem_rs)
            reducing()

        arrived(moves)
        grads = [
            jnp.concatenate([hal_g[slot, 0, comp], ghs[1 - step, comp], hal_g[slot, 1, comp]], axis=0)
            for comp in range(2)
        ]
        fresh = half_step_adjoint(speeds[0], speeds[1], grads)
        for comp in range(2):
            if step == 0:
                adj_out[comp] = fresh[comp][rows : 2 * rows]
            else:
                grid_g[comp] = fresh[comp]

    if IN_KERNEL_SUM:
        share_sum(count, pieces, scale, me, part, gathered, sum_out, sem_rs, sem_ag)
    else:
        sum_out[...] = part[...]
    for copy in started:
        copy.wait_send()


def scatter_sum(count, pieces, me, part, gathered, sem_rs):
    height = part.shape[0] // pieces

    def send(k, carry):
        peer = lax.rem(me + k, count)

        def go():
            pltpu.make_async_remote_copy(
                src_ref=part.at[pl.ds(pl.multiple_of(peer * height, height), height)],
                dst_ref=gathered.at[me],
                send_sem=sem_rs.at[0, k],
                recv_sem=sem_rs.at[1, me],
                device_id={"gx": peer},
                device_id_type=MESH,
            ).start()

        if pieces == count:
            go()
        else:
            pl.when(peer < pieces)(go)
        return carry

    lax.fori_loop(1, count, send, 0)


def share_sum(count, pieces, scale, me, part, gathered, sum_out, sem_rs, sem_ag):
    height = part.shape[0] // pieces

    def reduce_and_send():
        mine = pl.ds(pl.multiple_of(me * height, height), height)

        def add(k, acc):
            peer = lax.rem(me + k, count)
            pltpu.make_async_copy(gathered.at[peer], gathered.at[peer], sem_rs.at[1, peer]).wait()
            return acc + gathered[peer]

        sum_out[mine, :] = lax.fori_loop(1, count, add, part[mine, :]) * scale

        def send(k, carry):
            peer = lax.rem(me + k, count)
            pltpu.make_async_remote_copy(
                src_ref=sum_out.at[mine],
                dst_ref=sum_out.at[mine],
                send_sem=sem_ag.at[0, k],
                recv_sem=sem_ag.at[1, me],
                device_id={"gx": peer},
                device_id_type=MESH,
            ).start()
            return carry

        lax.fori_loop(1, count, send, 0)

        def sent(k, carry):
            pltpu.make_async_copy(gathered.at[0], gathered.at[0], sem_ag.at[0, k]).wait()
            return carry

        lax.fori_loop(1, count, sent, 0)

    if pieces == count:
        reduce_and_send()
    else:
        pl.when(me < pieces)(reduce_and_send)

    def finish(k, carry):
        peer = lax.rem(me + k, count)

        def go():
            pltpu.make_async_copy(gathered.at[0], gathered.at[0], sem_rs.at[0, k]).wait()
            spot = sum_out.at[pl.ds(pl.multiple_of(peer * height, height), height)]
            pltpu.make_async_copy(spot, spot, sem_ag.at[1, peer]).wait()

        if pieces == count:
            go()
        else:
            pl.when(peer < pieces)(go)
        return carry

    lax.fori_loop(1, count, finish, 0)


def on_device(states, pre_acts, cotangent, weight_in, weight_second, weight_third, weight_out):
    count = lax.axis_size("gx")
    rows, cols = cotangent.shape[1], cotangent.shape[2]
    ch = pre_acts.shape[3]
    taps = weight_in.shape[0]
    scale = 1.0 / math.sqrt(rows * count * cols)
    w_in = jnp.pad(jnp.transpose(weight_in.reshape(taps * ch, 2)), ((0, 14), (0, 0)))
    w_out = jnp.transpose(jnp.pad(weight_out, ((0, 0), (0, lane_pad - 2), (0, 0))).reshape(taps * lane_pad, ch))
    total_rows = 2 * ch + 8 + ch // 2
    pieces = total_rows // 8
    while pieces > count or total_rows % pieces:
        pieces //= 2
    tall = taps * ch
    vmem = pl.BlockSpec(memory_space=pltpu.VMEM)
    f32, bf16 = jnp.float32, jnp.bfloat16
    dma = pltpu.SemaphoreType.DMA
    adjoint, sums = pl.pallas_call(
        functools.partial(kernel, count, pieces, scale),
        out_shape=(
            jax.ShapeDtypeStruct(cotangent.shape, f32),
            jax.ShapeDtypeStruct((total_rows, cols), f32),
        ),
        in_specs=[vmem] * 7,
        out_specs=(vmem, vmem),
        scratch_shapes=[
            pltpu.VMEM((2, 2, 2, rows, cols), f32),
            pltpu.VMEM((3, 2, 2, rows, cols), f32),
            pltpu.VMEM((2, 2, ch, cols), bf16),
            pltpu.VMEM((4, 2, ch, cols), bf16),
            pltpu.VMEM((4, 2, ch, cols), bf16),
            pltpu.VMEM((2, 3 * rows, cols), f32),
            pltpu.VMEM(((rows + 4) * 24, cols), f32),
            pltpu.VMEM((2, (rows + 2) * 3 * ch, cols), bf16),
            pltpu.VMEM((rows * 16, cols), f32),
            pltpu.VMEM((2, 2, rows, cols), f32),
            pltpu.VMEM((total_rows, cols), f32),
            pltpu.VMEM((count, total_rows // pieces, cols), f32),
            pltpu.VMEM((ch, tall), bf16),
            pltpu.VMEM((ch, tall), bf16),
            dma((2, 2)),
            dma((3, 2, 2)),
            dma((2, 2, 2)),
            dma((4, 2, 2)),
            dma((2, count)),
            dma((2, count)),
        ],
        compiler_params=pltpu.CompilerParams(
            collective_id=0, has_side_effects=True, vmem_limit_bytes=48 * 1024 * 1024
        ),
    )(
        states,
        pre_acts,
        cotangent,
        w_in,
        weight_second.reshape(tall, ch),
        weight_third.reshape(tall, ch),
        w_out,
    )
    if not IN_KERNEL_SUM:
        sums = lax.psum(sums, "gx") * scale
    grad_second = jnp.transpose(sums[:ch, :tall]).reshape(taps, ch, ch)
    grad_third = jnp.transpose(sums[ch : 2 * ch, :tall]).reshape(taps, ch, ch)
    grad_in = jnp.transpose(sums[2 * ch : 2 * ch + 2, :tall]).reshape(taps, ch, 2)
    last = sums[2 * ch + 8 :]
    last = jnp.concatenate([last[:, : taps * lane_pad], last[:, 128 : 128 + taps * lane_pad]], axis=0)
    grad_out = jnp.transpose(last).reshape(taps, lane_pad, ch)[:, :2]
    return (adjoint, grad_in, grad_second, grad_third, grad_out)


def solution(mesh):
    return jax.shard_map(
        on_device,
        mesh=mesh,
        in_specs=(
            P(None, "groups", "gx", None),
            P(None, None, ("groups", "gx"), None, None),
            P("groups", "gx", None),
            P(),
            P(),
            P(),
            P(),
        ),
        out_specs=(
            P("groups", "gx", None),
            P("groups", None, None),
            P("groups", None, None),
            P("groups", None, None),
            P("groups", None, None),
        ),
        check_vma=False,
    )
```

time: 230 us -> 58.9 us (0.26)
  blocking collectives: 61.7 us -> 0 us
  starting transfers between devices: 56.4 us -> 0 us
  Pallas kernels: 0 us -> 46.8 us
  matrix products: 42.6 us -> 0 us
  waiting for transfers between devices: 32.5 us -> 0 us
  between operations: 15.5 us -> 0.67 us
  other arithmetic: 11.9 us -> 0.01 us
    psum x1 -> x0, blocking collectives: 61.7 us -> none  [on_device(): lax.psum((grad_totals[0], grad_totals[1], grad_totals[2], grad_totals[3])...]
    ppermute x24 -> x0, starting transfers between devices: 56.4 us -> none  [the longest x12 49.8 us: extended(): lax.ppermute(head, axis, [((i + 1) % count, i) for i in range(count)])]
    pallas_call x0 -> x1, Pallas kernels: none -> 46.8 us  [on_device(): pl.pallas_call(functools.partial(kernel, count, pieces, scale), out_shape...]
    dot_general x144 -> x0, matrix products: 42.6 us -> none  [the longest x72 23.2 us: back_conv(): jnp.einsum('ok,roy->rky', kernel[3 * row_tap + col_tap], section, preferr...]
    psum x1 -> x0, waiting for transfers between devices: 24.9 us -> none  [on_device(): lax.psum((grad_totals[0], grad_totals[1], grad_totals[2], grad_totals[3])...]
    ppermute x24 -> x0, waiting for transfers between devices: 7.57 us -> none  [the longest x12 6.63 us: extended(): lax.ppermute(tail, axis, [(i, (i + 1) % count) for i in range(count)])]
    unnamed x14 -> x13, local copies, waits for them, and re-layouts: 0.91 us -> 6.98 us
    mul x15 -> x0, other arithmetic: 4.93 us -> none  [the longest x1 1.64 us: on_device(): summed[2] * factor]
  transfers between devices with their start and end apart: 25 -> 0, of which waited for: 8 -> 0; matrix products, arithmetic and copies ran while one was open for 9% -> 0% of each run, Pallas kernels for 0% -> 0%
where the time goes in v1:
time: 58.9 us; the launch traced here: 57.8 us
  Pallas kernels  46.8 us (79%)
  local copies, waits for them, and re-layouts  10.3 us (17%)
  between operations  0.67 us (1%)
    pallas_call x1, Pallas kernels, on_device(): pl.pallas_call(functools.partial(kernel, count, pieces, scale), out_shape...  46.8 us
    unnamed x13, local copies, waits for them, and re-layouts  6.98 us

profile of v1, /device:TPU:1, one launch (start us, length us, event | category | flops | bytes accessed | tf_op | source)
XLA Modules:
  0.0 57.8 jit_solution(16984721234504731158)
XLA Ops:
  0.6 0.7 %copy.18 = bf16[9,48,2]{1,0,2:T(8,128)(2,1)S(1)} copy(bf16[9,48,2]{1,2,0:T(2,128)(2,1)} %param.10) | data formatting | bytes 3456 | tf_op args[3]
  1.3 0.1 reshape.34
  1.4 0.7 %pad_bitcast_fusion = bf16[72,48]{1,0:T(8,128)(2,1)S(1)} fusion(bf16[9,2,48]{2,1,0:T(2,128)(2,1)} %param.13), kind=kLoop, calls=%fused_computation.3 | loop fusion | bytes 8640 | tf_op jit(solution)/shard_map/reshape | solution.py:415
  2.1 0.1 copy.19
  2.2 0.0 copy-start
  2.2 1.7 %copy-done = bf16[2,3,8,48,512]{4,3,2,1,0:T(8,128)(2,1)S(1)} copy-done((bf16[2,3,8,48,512]{4,3,2,1,0:T(8,128)(2,1)S(1)}, bf16[2,3,8,48,512]{4,3,2,1,0:T(8,128)(2,1)}, u32[]{:S(2)}) %copy-start) | copy-done | bytes 2359320
  3.9 0.0 copy-start.1
  3.9 0.9 %copy-done.1 = bf16[9,48,48]{2,1,0:T(8,128)(2,1)S(1)} copy-done((bf16[9,48,48]{2,1,0:T(8,128)(2,1)S(1)}, bf16[9,48,48]{2,1,0:T(8,128)(2,1)}, u32[]{:S(2)}) %copy-start.1) | copy-done | bytes 41496
  4.8 0.0 copy-start.2
  4.8 0.9 %copy-done.2 = bf16[9,48,48]{2,1,0:T(8,128)(2,1)S(1)} copy-done((bf16[9,48,48]{2,1,0:T(8,128)(2,1)S(1)}, bf16[9,48,48]{2,1,0:T(8,128)(2,1)}, u32[]{:S(2)}) %copy-start.2) | copy-done | bytes 41496
  5.7 0.0 copy-start.3
  5.7 0.8 %copy-done.3 = f32[2,2,8,512]{3,2,1,0:T(8,128)S(1)} copy-done((f32[2,2,8,512]{3,2,1,0:T(8,128)S(1)}, f32[2,2,8,512]{3,2,1,0:T(8,128)}, u32[]{:S(2)}) %copy-start.3) | copy-done | bytes 65560
  6.5 0.0 copy-start.4
  6.5 0.8 %copy-done.4 = f32[2,8,512]{2,1,0:T(8,128)S(1)} copy-done((f32[2,8,512]{2,1,0:T(8,128)S(1)}, f32[2,8,512]{2,1,0:T(8,128)}, u32[]{:S(2)}) %copy-start.4) | copy-done | bytes 32792
  7.3 46.8 %shard_map.110 = (f32[2,8,512]{2,1,0:T(8,128)S(1)}, f32[128,512]{1,0:T(8,128)S(1)}) custom-call(f32[2,2,8,512]{3,2,1,0:T(8,128)S(1)} %copy-done.3, bf16[2,3,8,48,512]{4,3,2,1,0:T(8,128)(2,1)S(1)} %copy-done, f32[2,8,512]{2,1,0:T(8,128)S(1)} %copy-done.4, bf16[16,432]{1,0:T(8,128)(2,1)S(1)} %pad.8.w_in, bf16[432,48]{1,0:T(8,128)(2,1)S(1)} %bitcast.21, ...), custom_call_target="tpu_custom_call" | custom-call | tf_op jit(solution)/shard_map/pallas_call | solution.py:424
  54.1 0.1 reshape.38
  54.2 0.6 %copy.23 = f32[9,48,2]{1,2,0:T(2,128)} copy(f32[9,48,2]{1,0,2:T(8,128)S(1)} %reshape.38) | data formatting | bytes 6912
  54.8 0.1 copy.22
  54.9 0.6 %slice.27 = f32[9,2,48]{2,1,0:T(2,128)} slice(f32[9,8,48]{2,1,0:T(8,128)S(1)} %bitcast.26), slice={[0:9], [0:2], [0:48]} | slice | bytes 6912 | tf_op jit(solution)/shard_map/slice | solution.py:473
  55.5 0.8 %copy.21 = f32[432,48]{1,0:T(8,128)} copy(f32[432,48]{0,1:T(8,128)S(1)} %get-tuple-element.21) | data formatting | bytes 165888 | tf_op jit(solution)/shard_map/transpose | solution.py:469
  56.4 0.8 %copy.20 = f32[432,48]{1,0:T(8,128)} copy(f32[432,48]{0,1:T(8,128)S(1)} %get-tuple-element.22) | data formatting | bytes 165888 | tf_op jit(solution)/shard_map/transpose | solution.py:468
  57.2 0.6 %copy.25 = f32[2,8,512]{2,1,0:T(8,128)} copy(f32[2,8,512]{2,1,0:T(8,128)S(1)} %get-tuple-element.28) | data formatting | bytes 65536
  (5 shorter events, 0.0 us)
Async XLA Ops:
  2.2 1.7 %copy-start = (bf16[2,3,8,48,512]{4,3,2,1,0:T(8,128)(2,1)S(1)}, bf16[2,3,8,48,512]{4,3,2,1,0:T(8,128)(2,1)}, u32[]{:S(2)}) copy-start(bf16[2,3,8,48,512]{4,3,2,1,0:T(8,128)(2,1)} %acts.1) | copy-start | bytes 7077892
  3.9 0.9 %copy-start.1 = (bf16[9,48,48]{2,1,0:T(8,128)(2,1)S(1)}, bf16[9,48,48]{2,1,0:T(8,128)(2,1)}, u32[]{:S(2)}) copy-start(bf16[9,48,48]{2,1,0:T(8,128)(2,1)} %param.11) | copy-start | bytes 124420
  4.8 0.9 %copy-start.2 = (bf16[9,48,48]{2,1,0:T(8,128)(2,1)S(1)}, bf16[9,48,48]{2,1,0:T(8,128)(2,1)}, u32[]{:S(2)}) copy-start(bf16[9,48,48]{2,1,0:T(8,128)(2,1)} %param.12) | copy-start | bytes 124420
  5.7 0.8 %copy-start.3 = (f32[2,2,8,512]{3,2,1,0:T(8,128)S(1)}, f32[2,2,8,512]{3,2,1,0:T(8,128)}, u32[]{:S(2)}) copy-start(f32[2,2,8,512]{3,2,1,0:T(8,128)} %states.1) | copy-start | bytes 196612
  6.5 0.8 %copy-start.4 = (f32[2,8,512]{2,1,0:T(8,128)S(1)}, f32[2,8,512]{2,1,0:T(8,128)}, u32[]{:S(2)}) copy-start(f32[2,8,512]{2,1,0:T(8,128)} %cot.1) | copy-start | bytes 98308
